TPU v7x, 256 devices: a whole 4x4x8 slice. The times are simulated.
256 devices in a mesh: tgt: 64 (over x, z, core), rep: 4 (over y).
Axes of the slice: x: 4, y: 4, z: 8, core: 2. Of those that a mesh axis runs over, the one named last changes fastest.
Arguments:
- flux: bfloat16 [16384, 7808], P(('tgt', 'rep')), may hold values from 0.19921875 to 4
- ivar: bfloat16 [16384, 7808], P(('tgt', 'rep')), may hold values from 0.099609375 to 10
- row_target: int32 [16384], P(('tgt', 'rep')), may hold values from 0 to 8191, as said below
- start_w: float32 [8192, 64], P(('tgt', 'rep')), may hold values from 0.02 to 0.25
- start_h: float32 [64, 7808], P(None, 'tgt'), may hold values from 0.02 to 0.25
Outputs:
- activations: float32 [8192, 64], P(('tgt', 'rep'))
- templates: float32 [64, 7808], P(None, 'tgt')
Inputs may be any that keep to these rules, and one draw needn't show every extreme that they name: `row_target`: row i lies on device d = i // 64; its target t is owned by device t // 32, which has the same index along rep as d, i.e. (t // 32) % 4 == d % 4. The rows of one device name targets of one owning device at most 2 times, and every device reaches 2 for some owner. A target may have several rows or none.
All inputs are finite; a program needn't handle non-finite values.
Results may differ from a plain program's by a relative error of at most 0.035.
Values may be sent and summed in bfloat16 or wider, within the bound.
No kernel may reach another device: no remote copies, remote signals or barrier semaphores. Data moves between devices by JAX's collectives and lax.ppermute only.
A program may use at most 64 MiB of HBM per device.

v0:
```python
import jax
import jax.numpy as jnp
from jax import lax
from jax.sharding import PartitionSpec as P

SWEEPS = 2
PRIOR_IVAR = 0.5
EPSILON = 1e-06


def update_columns(activation, cross, gram):

    def column_step(index, current):
        gram_col = lax.dynamic_index_in_dim(gram, index, 1, keepdims=False)
        pivot = lax.dynamic_index_in_dim(gram_col, index, 0, keepdims=False)
        column = lax.dynamic_index_in_dim(current, index, 1, keepdims=False)
        wanted = lax.dynamic_index_in_dim(cross, index, 1, keepdims=False)
        fitted = jnp.dot(current, gram_col, precision=lax.Precision.HIGHEST)
        updated = jnp.maximum(column + (wanted - fitted) / (pivot + EPSILON), 0.0)
        return lax.dynamic_update_index_in_dim(current, updated, index, 1)

    return lax.fori_loop(0, activation.shape[1], column_step, activation)


def update_rows(templates, proj, gram):

    def row_step(index, current):
        gram_row = lax.dynamic_index_in_dim(gram, index, 0, keepdims=False)
        pivot = lax.dynamic_index_in_dim(gram_row, index, 0, keepdims=False)
        row_now = lax.dynamic_index_in_dim(current, index, 0, keepdims=False)
        wanted = lax.dynamic_index_in_dim(proj, index, 0, keepdims=False)
        fitted = jnp.dot(gram_row, current, precision=lax.Precision.HIGHEST)
        updated = jnp.maximum(row_now + (wanted - fitted) / (pivot + EPSILON), 0.0)
        return lax.dynamic_update_index_in_dim(current, updated, index, 0)

    return lax.fori_loop(0, templates.shape[0], row_step, templates)


def shards(flux, ivar, row_target, start_w, start_h):
    tgt_count = lax.axis_size("tgt")
    rep_count = lax.axis_size("rep")
    rows_dev = flux.shape[0]
    tgt_dev = start_w.shape[0]
    weighted = (ivar.astype(jnp.float32) * flux.astype(jnp.float32)).astype(jnp.bfloat16)
    owner_dev = row_target // tgt_dev
    peer_dev = owner_dev // rep_count
    capacity = 2 * rows_dev // tgt_count
    peer_onehot = (peer_dev[:, None] == jnp.arange(tgt_count, dtype=jnp.int32)[None, :]).astype(
        jnp.int32
    )
    running = jnp.cumsum(peer_onehot, axis=0)
    slot_index = jnp.sum(running * peer_onehot, axis=1) - 1
    place = peer_dev * capacity + slot_index
    source_row = (
        jnp.zeros((tgt_count * capacity,), jnp.int32)
        .at[place]
        .set(jnp.arange(rows_dev, dtype=jnp.int32))
    )
    filled = jnp.zeros((tgt_count * capacity,), jnp.int32).at[place].set(1)
    keep_rows = filled[:, None].astype(jnp.bfloat16)
    send_weighted = jnp.take(weighted, source_row, axis=0) * keep_rows
    send_ivar = jnp.take(ivar, source_row, axis=0) * keep_rows
    send_target = jnp.where(filled == 1, jnp.take(row_target, source_row, axis=0), -1)
    got_weighted, got_ivar, got_target = (
        lax.all_to_all(send_weighted, "tgt", split_axis=0, concat_axis=0, tiled=True),
        lax.all_to_all(send_ivar, "tgt", split_axis=0, concat_axis=0, tiled=True),
        lax.all_to_all(send_target, "tgt", split_axis=0, concat_axis=0, tiled=True),
    )
    first_target = (lax.axis_index("tgt") * rep_count + lax.axis_index("rep")) * tgt_dev
    selector = (
        got_target[None, :] - first_target == jnp.arange(tgt_dev, dtype=jnp.int32)[:, None]
    ).astype(jnp.bfloat16)
    numerator = jnp.dot(selector, got_weighted, preferred_element_type=jnp.float32)
    denominator = jnp.dot(selector, got_ivar, preferred_element_type=jnp.float32)
    coadd = (numerator / (denominator + PRIOR_IVAR)).astype(jnp.bfloat16)
    spectra = lax.all_to_all(coadd, "tgt", split_axis=1, concat_axis=0, tiled=True)
    activation = lax.all_gather(start_w, "tgt", axis=0, tiled=True)
    templates = start_h
    for sweep in range(SWEEPS):
        templ_bf = templates.astype(jnp.bfloat16)
        hgram_part = jnp.dot(templates, templates.T, precision=lax.Precision.HIGHEST)
        cross_part = jnp.dot(spectra, templ_bf.T, preferred_element_type=jnp.float32)
        cross, hgram = lax.psum((cross_part, hgram_part), "tgt")
        activation = update_columns(activation, cross, hgram)
        proj_part = lax.dot_general(
            activation.astype(jnp.bfloat16),
            spectra,
            (((0,), (0,)), ((), ())),
            preferred_element_type=jnp.float32,
        )
        wgram_part = jnp.dot(activation.T, activation, precision=lax.Precision.HIGHEST)
        proj, wgram = lax.psum((proj_part, wgram_part), "rep")
        templates = update_rows(templates, proj, wgram)
    own_w = lax.dynamic_slice_in_dim(activation, lax.axis_index("tgt") * tgt_dev, tgt_dev, 0)
    return (own_w, templates)


def solution(mesh):
    placed = (
        P(("tgt", "rep"), None),
        P(("tgt", "rep"), None),
        P(("tgt", "rep")),
        P(("tgt", "rep"), None),
        P(None, "tgt"),
    )
    return jax.shard_map(
        shards,
        mesh=mesh,
        in_specs=placed,
        out_specs=(P(("tgt", "rep"), None), P(None, "tgt")),
        check_vma=False,
    )
```

profile of v0, /device:TPU:8, one launch (start us, length us, event | category | flops | bytes accessed | tf_op | source)
XLA Modules:
  0.0 1318.5 jit_solution(9789575537605206230)
XLA Ops:
  10.4 1.6 gather_fusion
  13.6 11.9 all-to-all-start
  25.6 6.4 gather_fusion.2
  32.2 3.1 gather_fusion.1
  35.3 4.0 select_multiply_fusion.1
  39.4 1.7 all_to_all.41
  41.1 10.3 all-to-all-start.2
  51.4 5.0 all_to_all.38
  56.4 44.1 %all-to-all-done.2 = bf16[64,2,7808]{2,1,0:T(2,128)(2,1)S(1)} async-done(((bf16[64,2,7808]{2,1,0:T(2,128)(2,1)}), bf16[64,2,7808]{2,1,0:T(2,128)(2,1)S(1)}, u32[]{:S(2)}, u32[]{:S(2)}) %all-to-all-start.2) | async-done | bytes 1998880 | tf_op jit(solution)/shard_map/all_to_all | solution.py:66
  100.5 6.3 all-to-all-start.1
  107.1 4.3 all_to_all.43
  111.7 43.9 %all-to-all-done.1 = bf16[64,2,7808]{2,1,0:T(2,128)(2,1)} async-done(((bf16[64,2,7808]{2,1,0:T(2,128)(2,1)}), bf16[64,2,7808]{2,1,0:T(2,128)(2,1)}, u32[]{:S(2)}, u32[]{:S(2)}) %all-to-all-start.1) | async-done | bytes 1998880 | tf_op jit(solution)/shard_map/all_to_all | solution.py:65
  155.6 4.3 all_to_all.40
  160.3 2.1 all_to_all.44
  162.5 1.1 copy.17
  163.6 5.9 all-to-all-start.3
  169.5 17.1 %all-to-all-done.3 = bf16[32,64,122]{2,0,1:T(8,128)(2,1)S(1)} async-done(((bf16[32,64,122]{2,0,1:T(8,128)(2,1)}), bf16[32,64,122]{2,0,1:T(8,128)(2,1)S(1)}, u32[]{:S(2)}, u32[]{:S(2)}) %all-to-all-start.3) | async-done | bytes 499744 | tf_op jit(solution)/shard_map/all_to_all | solution.py:76
  186.7 1.1 fusion.28
  188.0 247.9 %psum.57 = f32[64,64]{1,0:T(8,128)S(1)} all-reduce(f32[64,64]{1,0:T(8,128)S(1)} %fusion.36), channel_id=1, replica_groups=mesh['tgt'=64,'rep'=4] {'tgt'}, use_global_device_ids=true, to_apply=%region_0.1 | all-reduce | flops 4096 | bytes 32768 | tf_op jit(solution)/shard_map/psum | solution.py:83
  436.0 47.2 %all_gather.3 = f32[2048,64]{1,0:T(8,128)S(1)} all-gather(f32[32,64]{1,0:T(8,128)S(1)} %copy-done.4), channel_id=1, replica_groups=mesh['tgt'=64,'rep'=4] {'tgt'}, dimensions={0}, use_global_device_ids=true | all-gather | bytes 532480 | tf_op jit(solution)/shard_map/all_gather | solution.py:77
  483.5 181.6 %while.64 = (s32[]{:T(128)}, f32[2048,64]{0,1:T(8,128)S(1)}, f32[2048,64]{0,1:T(8,128)}, f32[64,64]{0,1:T(8,128)S(1)}, s32[]{:T(128)}, /*index=5*/s32[]{:T(128)}, s32[]{:T(128)}, f32[1,1]{0,1:T(1,128)}) while((s32[]{:T(128)}, f32[2048,64]{0,1:T(8,128)S(1)}, f32[2048,64]{0,1:T(8,128)}, f32[64,64]{0,1:T(8,128)S(1)}, s32[]{:T(128)}, ...), condition=%wide.region_7.9_spmd, body=%wide.region_6.8_spmd.sunk | while | flops 1581060 | bytes 615053 | solution.py:22
  483.5 0.9 constant_dynamic-slice_fusion.20
  486.4 0.9 constant_dynamic-slice_fusion.20
  497.7 0.9 constant_dynamic-slice_fusion.20
  500.6 0.9 constant_dynamic-slice_fusion.20
  665.9 14.8 %all-reduce.1 = (f32[64,122]{1,0:T(8,128)S(1)}, f32[64,64]{1,0:T(8,128)S(1)}) all-reduce(f32[64,122]{1,0:T(8,128)S(1)} %fusion.23, f32[64,64]{1,0:T(8,128)S(1)} %fusion.37), channel_id=1, replica_groups=mesh['tgt'=64,'rep'=4] {'rep'}, use_global_device_ids=true, to_apply=%region_9.11 | all-reduce | flops 11904 | bytes 95232 | tf_op jit(solution)/shard_map/psum | solution.py:92
  680.7 91.4 %while.65 = (s32[]{:T(128)}, f32[64,122]{1,0:T(8,128)S(1)}, f32[64,122]{1,0:T(8,128)S(1)}, f32[64,64]{1,0:T(8,128)S(1)}, s32[]{:T(128)}, /*index=5*/s32[]{:T(128)}, s32[]{:T(128)}, f32[1,1]{1,0:T(1,128)}) while((s32[]{:T(128)}, f32[64,122]{1,0:T(8,128)S(1)}, f32[64,122]{1,0:T(8,128)S(1)}, f32[64,64]{1,0:T(8,128)S(1)}, s32[]{:T(128)}, ...), condition=%wide.region_11.13_spmd, body=%wide.region_10.12_spmd.sunk | while | flops 94188 | bytes 37433 | solution.py:36
  772.2 1.1 fusion.26
  773.5 246.2 %psum.61 = f32[64,64]{1,0:T(8,128)S(1)} all-reduce(f32[64,64]{1,0:T(8,128)S(1)} %fusion.38), channel_id=1, replica_groups=mesh['tgt'=64,'rep'=4] {'tgt'}, use_global_device_ids=true, to_apply=%region_12.14 | all-reduce | flops 4096 | bytes 32768 | tf_op jit(solution)/shard_map/psum | solution.py:83
  1019.7 181.6 %while.66 = (s32[]{:T(128)}, f32[2048,64]{0,1:T(8,128)S(1)}, f32[2048,64]{0,1:T(8,128)}, f32[64,64]{0,1:T(8,128)S(1)}, s32[]{:T(128)}, /*index=5*/s32[]{:T(128)}, s32[]{:T(128)}, f32[1,1]{0,1:T(1,128)}) while((s32[]{:T(128)}, f32[2048,64]{0,1:T(8,128)S(1)}, f32[2048,64]{0,1:T(8,128)}, f32[64,64]{0,1:T(8,128)S(1)}, s32[]{:T(128)}, ...), condition=%wide.region_15.17_spmd, body=%wide.region_14.16_spmd.sunk | while | flops 1581060 | bytes 615053 | solution.py:22
  1202.4 17.2 %all-reduce = (f32[64,122]{1,0:T(8,128)S(1)}, f32[64,64]{1,0:T(8,128)S(1)}) all-reduce(f32[64,122]{1,0:T(8,128)S(1)} %fusion.21, f32[64,64]{1,0:T(8,128)S(1)} %fusion.39), channel_id=1, replica_groups=mesh['tgt'=64,'rep'=4] {'rep'}, use_global_device_ids=true, to_apply=%region_17.19 | all-reduce | flops 11904 | bytes 95232 | tf_op jit(solution)/shard_map/psum | solution.py:92
  1219.7 91.4 %while.67 = (s32[]{:T(128)}, f32[64,122]{1,0:T(8,128)S(1)}, f32[64,122]{1,0:T(8,128)S(1)}, f32[64,64]{1,0:T(8,128)S(1)}, s32[]{:T(128)}, /*index=5*/s32[]{:T(128)}, s32[]{:T(128)}, f32[1,1]{1,0:T(1,128)}) while((s32[]{:T(128)}, f32[64,122]{1,0:T(8,128)S(1)}, f32[64,122]{1,0:T(8,128)S(1)}, f32[64,64]{1,0:T(8,128)S(1)}, s32[]{:T(128)}, ...), condition=%wide.region_19.21_spmd, body=%wide.region_18.20_spmd.sunk | while | flops 94188 | bytes 37433 | solution.py:36
  (1067 shorter events, 372.9 us)
Async XLA Ops:
  13.6 27.5 %all-to-all-start = ((s32[64,2,1]{1,2,0:T(1,128)}), s32[64,2,1]{1,2,0:T(1,128)S(1)}, u32[]{:S(2)}, u32[]{:S(2)}) async-start(s32[64,2,1]{1,2,0:T(1,128)} %bitcast.26), calls=%async_computation | async-start | bytes 65536 | tf_op jit(solution)/shard_map/all_to_all | solution.py:67
  25.5 6.4 copy-start
  25.5 6.4 copy-start.3
  41.1 59.4 %all-to-all-start.2 = ((bf16[64,2,7808]{2,1,0:T(2,128)(2,1)}), bf16[64,2,7808]{2,1,0:T(2,128)(2,1)S(1)}, u32[]{:S(2)}, u32[]{:S(2)}) async-start(bf16[64,2,7808]{2,1,0:T(2,128)(2,1)} %all_to_all.41), calls=%async_computation.2 | async-start | bytes 3997696 | tf_op jit(solution)/shard_map/all_to_all | solution.py:66
  100.5 6.3 copy-start.2
  100.5 55.1 %all-to-all-start.1 = ((bf16[64,2,7808]{2,1,0:T(2,128)(2,1)}), bf16[64,2,7808]{2,1,0:T(2,128)(2,1)}, u32[]{:S(2)}, u32[]{:S(2)}) async-start(bf16[64,2,7808]{2,1,0:T(2,128)(2,1)} %all_to_all.38), calls=%async_computation.1 | async-start | bytes 3997696 | tf_op jit(solution)/shard_map/all_to_all | solution.py:65
  162.4 273.6 %copy-start.4 = (f32[32,64]{1,0:T(8,128)S(1)}, f32[32,64]{1,0:T(8,128)}, u32[]{:S(2)}) copy-start(f32[32,64]{1,0:T(8,128)} %param.18) | copy-start | bytes 24580
  163.6 23.1 %all-to-all-start.3 = ((bf16[32,64,122]{2,0,1:T(8,128)(2,1)}), bf16[32,64,122]{2,0,1:T(8,128)(2,1)S(1)}, u32[]{:S(2)}, u32[]{:S(2)}) async-start(bf16[32,64,122]{2,0,1:T(8,128)(2,1)} %copy.17), calls=%async_computation.3 | async-start | bytes 1048576 | tf_op jit(solution)/shard_map/all_to_all | solution.py:76
  169.5 314.1 %all-reduce.5.cloned.1.call-start = ((), (), s32[]{:S(2)}) async-start(), calls=%async_computation.4 | async-start | bytes 1048576 | tf_op jit(solution)/shard_map/psum | solution.py:83
  187.8 831.9 %all-reduce.7.cloned.1.call-start = ((), (), s32[]{:S(2)}) async-start(), calls=%async_computation.5 | async-start | bytes 1048576 | tf_op jit(solution)/shard_map/psum | solution.py:83
  1311.1 0.6 copy-start.1
Sparse Core Ops, SparseCore 0:
  187.9 178.6 all-reduce.4
  773.4 179.9 all-reduce.6
where the time goes:
time: 1330 us; the launch traced here: 1320 us
  blocking collectives  573 us (43%)
  local copies, waits for them, and re-layouts  335 us (25%)
  loops' own time  179 us (13%)
  waiting for transfers between devices  105 us (8%)
  matrix products  70.2 us (5%)
  starting transfers between devices  34.5 us (3%)
  between operations  14.4 us (1%)
    psum x2, blocking collectives, shards(): cross, hgram = lax.psum((cross_part, hgram_part), 'tgt')  494 us
    dynamic_slice x128, local copies, waits for them, and re-layouts, column_step(): wanted = lax.dynamic_index_in_dim(cross, index, 1, keepdims=False)  110 us
    another operation x2, loops' own time, update_columns(): return lax.fori_loop(0, activation.shape[1], column_step, activation)  93.4 us
    dynamic_slice x128, local copies, waits for them, and re-layouts, column_step(): pivot = lax.dynamic_index_in_dim(gram_col, index, 0, keepdims=False)  85.8 us
    another operation x2, loops' own time, update_rows(): return lax.fori_loop(0, templates.shape[0], row_step, templates)  85.8 us
    dynamic_slice x128, local copies, waits for them, and re-layouts, row_step(): pivot = lax.dynamic_index_in_dim(gram_row, index, 0, keepdims=False)  75.3 us
    all_gather x1, blocking collectives, shards(): activation = lax.all_gather(start_w, 'tgt', axis=0, tiled=True)  47.2 us
    dot_general x128, matrix products, column_step(): fitted = jnp.dot(current, gram_col, precision=lax.Precision.HIGHEST)  46.8 us
  transfers between devices with their start and end apart: 6, of which 3 were waited for; matrix products, arithmetic and copies ran while one was open for 1% of the time, Pallas kernels for 0%

commit v1 on v0

--- a/solution.py
+++ b/solution.py
@@ -6,6 +6,24 @@
 SWEEPS = 2
 PRIOR_IVAR = 0.5
 EPSILON = 1e-06
+
+
+def in_order(blocks, dim):
+    blocks = jnp.moveaxis(blocks, 0, dim)
+    shape = blocks.shape
+    return blocks.reshape(*shape[:dim], shape[dim] * shape[dim + 1], *shape[dim + 2 :])
+
+
+def collected_by_bits(x, axis):
+    size = lax.axis_size(axis)
+    parts = x[None]
+    for level in range(size.bit_length() - 1):
+        distance = 1 << level
+        other = lax.ppermute(parts, axis, [(i, i ^ distance) for i in range(size)])
+        both = jnp.stack([parts, other])
+        upper = lax.axis_index(axis) >> level & 1
+        parts = jnp.where(upper == 0, both, both[::-1]).reshape(-1, *x.shape)
+    return parts
 
 
 def update_columns(activation, cross, gram):
@@ -74,7 +92,7 @@
     denominator = jnp.dot(selector, got_ivar, preferred_element_type=jnp.float32)
     coadd = (numerator / (denominator + PRIOR_IVAR)).astype(jnp.bfloat16)
     spectra = lax.all_to_all(coadd, "tgt", split_axis=1, concat_axis=0, tiled=True)
-    activation = lax.all_gather(start_w, "tgt", axis=0, tiled=True)
+    activation = in_order(collected_by_bits(start_w, "tgt"), 0)
     templates = start_h
     for sweep in range(SWEEPS):
         templ_bf = templates.astype(jnp.bfloat16)

time: 1330 us -> 1470 us (1.11)
  waiting for transfers between devices: 105 us -> 285 us
  blocking collectives: 573 us -> 526 us
  starting transfers between devices: 34.5 us -> 49.5 us
    psum x2, waiting for transfers between devices: 0.04 us -> 175 us  [shards(): cross, hgram = lax.psum((cross_part, hgram_part), 'tgt')]
    ppermute x0 -> x6, waiting for transfers between devices: none -> 66.2 us  [collected_by_bits(): other = lax.ppermute(parts, axis, [(i, i ^ distance) for i in range(size)])]
    all_gather x1 -> x0, blocking collectives: 47.2 us -> none  [shards(): activation = lax.all_gather(start_w, 'tgt', axis=0, tiled=True)]
    all_to_all x1, waiting for transfers between devices: 43.9 us -> 0.01 us  [shards(): lax.all_to_all(send_weighted, 'tgt', split_axis=0, concat_axis=0, tiled=T...]
    all_to_all x1, waiting for transfers between devices: 17.1 us -> 0.01 us  [shards(): lax.all_to_all(coadd, 'tgt', split_axis=1, concat_axis=0, tiled=True)]
  transfers between devices with their start and end apart: 6 -> 12, of which waited for: 3 -> 7; matrix products, arithmetic and copies ran while one was open for 1% -> 1% of each run, Pallas kernels for 0% -> 0%
where the time goes in v1:
time: 1470 us
  blocking collectives  526 us (36%)
  local copies, waits for them, and re-layouts  333 us (23%)
  waiting for transfers between devices  285 us (19%)
  loops' own time  178 us (12%)
  matrix products  72.3 us (5%)
  starting transfers between devices  49.5 us (3%)
    psum x2, blocking collectives, shards(): cross, hgram = lax.psum((cross_part, hgram_part), 'tgt')  494 us
    psum x2, waiting for transfers between devices, shards(): cross, hgram = lax.psum((cross_part, hgram_part), 'tgt')  175 us
    dynamic_slice x128, local copies, waits for them, and re-layouts, column_step(): wanted = lax.dynamic_index_in_dim(cross, index, 1, keepdims=False)  110 us
    another operation x2, loops' own time, update_columns(): return lax.fori_loop(0, activation.shape[1], column_step, activation)  91.8 us
    another operation x2, loops' own time, update_rows(): return lax.fori_loop(0, templates.shape[0], row_step, templates)  85.8 us
    dynamic_slice x128, local copies, waits for them, and re-layouts, column_step(): pivot = lax.dynamic_index_in_dim(gram_col, index, 0, keepdims=False)  83.7 us
    dynamic_slice x128, local copies, waits for them, and re-layouts, row_step(): pivot = lax.dynamic_index_in_dim(gram_row, index, 0, keepdims=False)  75.3 us
    ppermute x6, waiting for transfers between devices, collected_by_bits(): other = lax.ppermute(parts, axis, [(i, i ^ distance) for i in range(size)])  66.2 us
  transfers between devices with their start and end apart: 12, of which 7 were waited for; matrix products, arithmetic and copies ran while one was open for 1% of the time, Pallas kernels for 0%

profile of v1, /device:TPU:8, one launch (start us, length us, event | category | flops | bytes accessed | tf_op | source)
XLA Modules:
  0.0 1465.5 jit_solution(15227096732878844923)
XLA Ops:
  10.4 1.6 gather_fusion
  13.6 11.9 all-to-all-start
  25.6 6.4 gather_fusion.2
  32.2 3.2 gather_fusion.1
  35.4 4.1 select_multiply_fusion.1
  39.5 1.7 all_to_all.41
  41.2 10.3 all-to-all-start.2
  51.5 5.0 all_to_all.38
  56.6 44.1 %all-to-all-done.2 = bf16[64,2,7808]{2,1,0:T(2,128)(2,1)S(1)} async-done(((bf16[64,2,7808]{2,1,0:T(2,128)(2,1)}), bf16[64,2,7808]{2,1,0:T(2,128)(2,1)S(1)}, u32[]{:S(2)}, u32[]{:S(2)}) %all-to-all-start.2) | async-done | bytes 1998880 | tf_op jit(solution)/shard_map/all_to_all | solution.py:84
  100.6 6.1 all-to-all-start.1
  108.1 1.8 collective-permute-start.1
  109.8 42.5 %collective-permute-done.1 = f32[2,32,64]{2,1,0:T(8,128)S(1)} collective-permute-done((f32[2,32,64]{2,1,0:T(8,128)S(1)}, f32[2,32,64]{2,1,0:T(8,128)S(1)}, u32[]{:S(2)}, u32[]{:S(2)}) %collective-permute-start.1) | collective-permute-done | bytes 16416 | tf_op jit(solution)/shard_map/ppermute | solution.py:22
  153.6 5.0 collective-permute-done.2
  158.6 5.1 collective-permute-start.3
  164.0 6.7 collective-permute-done.3
  170.7 4.3 all_to_all.43
  176.3 4.3 all_to_all.40
  180.6 1.6 fusion.20
  182.2 2.1 all_to_all.44
  185.5 8.1 all-to-all-start.3
  193.7 1.7 collective-permute-start.4
  195.4 10.8 collective-permute-done.4
  206.3 3.0 collective-permute-start.5
  209.5 248.3 %psum.57 = f32[64,64]{1,0:T(8,128)S(1)} all-reduce(f32[64,64]{1,0:T(8,128)S(1)} %fusion.38), channel_id=1, replica_groups=mesh['tgt'=64,'rep'=4] {'tgt'}, use_global_device_ids=true, to_apply=%region_0.1 | all-reduce | flops 4096 | bytes 32768 | tf_op jit(solution)/shard_map/psum | solution.py:101
  459.6 174.8 %all-reduce.5.cloned.1.call-done = f32[2048,64]{0,1:T(8,128)} async-done(((f32[2048,64]{0,1:T(8,128)}), f32[2048,64]{0,1:T(8,128)}) %all-reduce.5.cloned.1.call-update) | async-done | bytes 524304 | tf_op jit(solution)/shard_map/psum | solution.py:101
  634.3 179.7 %while.64 = (s32[]{:T(128)}, f32[2048,64]{0,1:T(8,128)S(1)}, f32[2048,64]{0,1:T(8,128)}, f32[64,64]{0,1:T(8,128)S(1)}, s32[]{:T(128)}, /*index=5*/s32[]{:T(128)}, s32[]{:T(128)}, f32[1,1]{0,1:T(1,128)}) while((s32[]{:T(128)}, f32[2048,64]{0,1:T(8,128)S(1)}, f32[2048,64]{0,1:T(8,128)}, f32[64,64]{0,1:T(8,128)S(1)}, s32[]{:T(128)}, ...), condition=%wide.region_7.9_spmd, body=%wide.region_6.8_spmd.sunk | while | flops 1581060 | bytes 615053 | solution.py:40
  814.9 14.6 all-reduce.1
  829.5 91.4 %while.65 = (s32[]{:T(128)}, f32[64,122]{1,0:T(8,128)S(1)}, f32[64,122]{1,0:T(8,128)S(1)}, f32[64,64]{1,0:T(8,128)S(1)}, s32[]{:T(128)}, /*index=5*/s32[]{:T(128)}, s32[]{:T(128)}, f32[1,1]{1,0:T(1,128)}) while((s32[]{:T(128)}, f32[64,122]{1,0:T(8,128)S(1)}, f32[64,122]{1,0:T(8,128)S(1)}, f32[64,64]{1,0:T(8,128)S(1)}, s32[]{:T(128)}, ...), condition=%wide.region_11.13_spmd, body=%wide.region_10.12_spmd.sunk | while | flops 94188 | bytes 37433 | solution.py:54
  922.2 246.2 %psum.61 = f32[64,64]{1,0:T(8,128)S(1)} all-reduce(f32[64,64]{1,0:T(8,128)S(1)} %fusion.40), channel_id=1, replica_groups=mesh['tgt'=64,'rep'=4] {'tgt'}, use_global_device_ids=true, to_apply=%region_12.14 | all-reduce | flops 4096 | bytes 32768 | tf_op jit(solution)/shard_map/psum | solution.py:101
  1168.5 179.7 %while.66 = (s32[]{:T(128)}, f32[2048,64]{0,1:T(8,128)S(1)}, f32[2048,64]{0,1:T(8,128)}, f32[64,64]{0,1:T(8,128)S(1)}, s32[]{:T(128)}, /*index=5*/s32[]{:T(128)}, s32[]{:T(128)}, f32[1,1]{0,1:T(1,128)}) while((s32[]{:T(128)}, f32[2048,64]{0,1:T(8,128)S(1)}, f32[2048,64]{0,1:T(8,128)}, f32[64,64]{0,1:T(8,128)S(1)}, s32[]{:T(128)}, ...), condition=%wide.region_15.17_spmd, body=%wide.region_14.16_spmd.sunk | while | flops 1581060 | bytes 615053 | solution.py:40
  1349.3 17.3 %all-reduce = (f32[64,122]{1,0:T(8,128)S(1)}, f32[64,64]{1,0:T(8,128)S(1)}) all-reduce(f32[64,122]{1,0:T(8,128)S(1)} %fusion.21, f32[64,64]{1,0:T(8,128)S(1)} %fusion.41), channel_id=1, replica_groups=mesh['tgt'=64,'rep'=4] {'rep'}, use_global_device_ids=true, to_apply=%region_17.19 | all-reduce | flops 11904 | bytes 95232 | tf_op jit(solution)/shard_map/psum | solution.py:110
  1366.6 91.4 %while.67 = (s32[]{:T(128)}, f32[64,122]{1,0:T(8,128)S(1)}, f32[64,122]{1,0:T(8,128)S(1)}, f32[64,64]{1,0:T(8,128)S(1)}, s32[]{:T(128)}, /*index=5*/s32[]{:T(128)}, s32[]{:T(128)}, f32[1,1]{1,0:T(1,128)}) while((s32[]{:T(128)}, f32[64,122]{1,0:T(8,128)S(1)}, f32[64,122]{1,0:T(8,128)S(1)}, f32[64,64]{1,0:T(8,128)S(1)}, s32[]{:T(128)}, ...), condition=%wide.region_19.21_spmd, body=%wide.region_18.20_spmd.sunk | while | flops 94188 | bytes 37433 | solution.py:54
  (1090 shorter events, 381.0 us)
Async XLA Ops:
  13.6 27.6 %all-to-all-start = ((s32[64,2,1]{1,2,0:T(1,128)}), s32[64,2,1]{1,2,0:T(1,128)S(1)}, u32[]{:S(2)}, u32[]{:S(2)}) async-start(s32[64,2,1]{1,2,0:T(1,128)} %bitcast.45), calls=%async_computation | async-start | bytes 65536 | tf_op jit(solution)/shard_map/all_to_all | solution.py:85
  25.5 6.5 copy-start
  25.5 6.4 copy-start.3
  41.2 59.4 %all-to-all-start.2 = ((bf16[64,2,7808]{2,1,0:T(2,128)(2,1)}), bf16[64,2,7808]{2,1,0:T(2,128)(2,1)S(1)}, u32[]{:S(2)}, u32[]{:S(2)}) async-start(bf16[64,2,7808]{2,1,0:T(2,128)(2,1)} %all_to_all.41), calls=%async_computation.2 | async-start | bytes 3997696 | tf_op jit(solution)/shard_map/all_to_all | solution.py:84
  56.6 50.2 %copy-start.4 = (f32[32,64]{1,0:T(8,128)S(1)}, f32[32,64]{1,0:T(8,128)}, u32[]{:S(2)}) copy-start(f32[32,64]{1,0:T(8,128)} %param.18) | copy-start | bytes 24580
  100.6 6.1 copy-start.2
  100.6 75.7 %all-to-all-start.1 = ((bf16[64,2,7808]{2,1,0:T(2,128)(2,1)}), bf16[64,2,7808]{2,1,0:T(2,128)(2,1)}, u32[]{:S(2)}, u32[]{:S(2)}) async-start(bf16[64,2,7808]{2,1,0:T(2,128)(2,1)} %all_to_all.38), calls=%async_computation.1 | async-start | bytes 3997696 | tf_op jit(solution)/shard_map/all_to_all | solution.py:83
  106.8 1.3 collective-permute-start
  108.1 44.3 %collective-permute-start.1 = (f32[2,32,64]{2,1,0:T(8,128)S(1)}, f32[2,32,64]{2,1,0:T(8,128)S(1)}, u32[]{:S(2)}, u32[]{:S(2)}) collective-permute-start(f32[2,32,64]{2,1,0:T(8,128)S(1)} %get-tuple-element.578), channel_id=1, source_target_pairs={{0,8},{4,12},{8,0},{12,4},{16,24},{20,28},{24,16},{28,20},{32,40},... | collective-permute-start | bytes 49160 | tf_op jit(solution)/shard_map/ppermute | solution.py:22
  152.3 6.2 collective-permute-start.2
  158.6 12.1 collective-permute-start.3
  185.5 272.5 %all-to-all-start.3 = ((bf16[32,64,122]{2,0,1:T(8,128)(2,1)}), bf16[32,64,122]{2,0,1:T(8,128)(2,1)S(1)}, u32[]{:S(2)}, u32[]{:S(2)}) async-start(bf16[32,64,122]{2,0,1:T(8,128)(2,1)} %copy.23), calls=%async_computation.3 | async-start | bytes 1048576 | tf_op jit(solution)/shard_map/all_to_all | solution.py:94
  193.6 440.7 %all-reduce.5.cloned.1.call-start = ((), (), s32[]{:S(2)}) async-start(), calls=%async_computation.4 | async-start | bytes 1048576 | tf_op jit(solution)/shard_map/psum | solution.py:101
  193.7 12.5 collective-permute-start.4
  206.3 251.5 %collective-permute-start.5 = (f32[32,32,64]{2,1,0:T(8,128)S(1)}, f32[32,32,64]{2,1,0:T(8,128)S(1)}, u32[]{:S(2)}, u32[]{:S(2)}) collective-permute-start(f32[32,32,64]{2,1,0:T(8,128)S(1)} %bitcast.166), channel_id=1, source_target_pairs={{0,128},{4,132},{8,136},{12,140},{16,144},{20,148},{24,152},{28,15... | collective-permute-start | bytes 786440 | tf_op jit(solution)/shard_map/ppermute | solution.py:22
  459.1 709.4 %all-reduce.7.cloned.1.call-start = ((), (), s32[]{:S(2)}) async-start(), calls=%async_computation.5 | async-start | bytes 1048576 | tf_op jit(solution)/shard_map/psum | solution.py:101
  1458.0 0.6 copy-start.1
Sparse Core Ops, SparseCore 0:
  459.2 175.1 all-reduce.4
  922.1 180.2 all-reduce.6
